TPU v7x, 32 devices: a whole 2x2x4 slice. The times are simulated.
32 devices in a mesh: narrow: 4 (over y, x), wide: 8 (over z, core).
Axes of the slice: x: 2, y: 2, z: 4, core: 2. Of those that a mesh axis runs over, the one named last changes fastest.
Arguments:
- hidden_in: bfloat16 [32768, 768], P(('narrow', 'wide')), may hold values from -6 to 6
- norm_gain_one: float32 [768], replicated, may hold values from 0.5 to 1.5
- w_qkv: bfloat16 [768, 2304], replicated, may hold values from -0.21875 to 0.21875
- w_out: bfloat16 [768, 768], replicated, may hold values from -0.875 to 0.875
- pos_table: float32 [32, 12], replicated, may hold values from -4 to 4
- norm_gain_two: float32 [768], replicated, may hold values from 0.5 to 1.5
- w_router: bfloat16 [768, 32], replicated, may hold values from -0.08984375 to 0.08984375
- w_in: bfloat16 [32, 768, 3072], P(('narrow', 'wide')), may hold values from -0.21875 to 0.21875
- w_down: bfloat16 [32, 3072, 768], P(('narrow', 'wide')), may hold values from -3.453125 to 3.453125
- expert_ids: int32 [32768, 1], P(('narrow', 'wide')), may hold values from 0 to 31
- segment_ids: int32 [64, 512], P(('narrow', 'wide')), may hold values from 0 to 3, never falling along the last dimension, each value on 1 to 256 neighbouring positions
- rel_buckets: int32 [512, 512], replicated, may hold values from 0 to 31
- out_grad: bfloat16 [32768, 768], P(('narrow', 'wide')), may hold values from -6 to 6
Outputs:
- layer_out: bfloat16 [32768, 768], P(('narrow', 'wide'))
- in_grad: float32 [32768, 768], P(('narrow', 'wide'))
- gain_one_grad: float32 [768], replicated
- qkv_grad: float32 [768, 2304], replicated
- out_proj_grad: float32 [768, 768], replicated
- table_grad: float32 [32, 12], replicated
- gain_two_grad: float32 [768], replicated
- router_grad: float32 [768, 32], replicated
- w_in_grad: float32 [32, 768, 3072], P(('narrow', 'wide'))
- w_down_grad: float32 [32, 3072, 768], P(('narrow', 'wide'))
Inputs may be any that keep to these rules, and one draw needn't show every extreme that they name: `segment_ids`: document numbers never fall along a row.
All inputs are finite; a program needn't handle non-finite values.
Results may differ from a plain program's by a relative error of at most 0.015.
Values may be sent and summed in bfloat16 or wider, within the bound.
A program may use at most 256 MiB of HBM per device.

v0:
```python
import functools
import jax
import jax.numpy as jnp
from jax import lax
from jax.experimental import pallas as pl
from jax.experimental.pallas import tpu as pltpu
from jax.sharding import PartitionSpec as P

HEADS = 12
HEAD_DIM = 64
LEN = 512
BUCKETS = 32
EPS = 1e-06
LANES = 128
HALF = 256
GROUP = 4
PAIR = 2
GROUPS = HEADS // GROUP
GW = GROUP * HEAD_DIM
F32 = jnp.float32
BF16 = jnp.bfloat16
MIB = 1024 * 1024
MICRO = 1150000000


def dot_nn(a, b):
    return lax.dot_general(a, b, (((1,), (0,)), ((), ())), preferred_element_type=F32)


def dot_tn(a, b):
    return lax.dot_general(a, b, (((0,), (0,)), ((), ())), preferred_element_type=F32)


def dot_nt(a, b):
    return lax.dot_general(a, b, (((1,), (1,)), ((), ())), preferred_element_type=F32)


def whole(shape):
    rank = len(shape)
    return pl.BlockSpec(shape, lambda *g: (0,) * rank, pipeline_mode=pl.Buffered(1))


def split3(v):
    high = v.astype(BF16)
    rest = v - high.astype(F32)
    mid = rest.astype(BF16)
    low = (rest - mid.astype(F32)).astype(BF16)
    return high, mid, low


def slots_kernel(experts, cap, capp, ids_ref, g_ref, slot_ref, pos_ref, packed_ref):
    tok = ids_ref.shape[1]
    ids = ids_ref[...]
    hot = lax.broadcasted_iota(jnp.int32, (experts, tok), 0) == ids
    before = (
        lax.broadcasted_iota(jnp.int32, (tok, tok), 0)
        < lax.broadcasted_iota(jnp.int32, (tok, tok), 1)
    )
    counts = dot_nn(hot.astype(F32).astype(BF16), before.astype(F32).astype(BF16))
    pos = jnp.sum(jnp.where(hot, counts, 0.0), axis=0, keepdims=True).astype(jnp.int32)
    kept = pos < cap
    slot = jnp.where(kept, ids * capp + pos, -1)
    slot_ref[...] = slot
    pos_ref[...] = jnp.where(kept, pos, -1)
    rows = packed_ref.shape[0]
    step = 256

    @pl.loop(0, rows // step)
    def _(r):
        base = pl.multiple_of(r * step, step)
        table = (lax.broadcasted_iota(jnp.int32, (step, tok), 0) + base == slot)
        packed_ref[pl.ds(base, step), :] = dot_nn(
            table.astype(F32).astype(BF16), g_ref[...]
        ).astype(BF16)


def make_slots(experts, cap, capp, ids_row, g):
    tok, width = g.shape
    return pl.pallas_call(
        functools.partial(slots_kernel, experts, cap, capp),
        out_shape=(
            jax.ShapeDtypeStruct((1, tok), jnp.int32),
            jax.ShapeDtypeStruct((1, tok), jnp.int32),
            jax.ShapeDtypeStruct((experts * capp, width), BF16),
        ),
        compiler_params=pltpu.CompilerParams(vmem_limit_bytes=40 * MIB),
        cost_estimate=pl.CostEstimate(flops=5 * MICRO, bytes_accessed=4 * MIB, transcendentals=0),
        name="slots",
    )(ids_row, g)


def column(row_ref):
    row = row_ref[...]
    return jnp.broadcast_to(row, (8, row.shape[1])).T[:, :1]


def front_kernel(
    hid_ref, gain1_ref, wq_ref, wk_ref, wv_ref, wout_ref, tab_ref, gain2_ref, wr_ref,
    ids_ref, slot_ref, pos_ref, segr_ref, rel_ref,
    n1_ref, q_ref, k_ref, v_ref, p_ref, attn_ref, resid_ref, n2_ref, route_ref, gate_ref,
    packed_ref, gpack_ref,
    relt, mask, bias, lines,
):
    step = pl.program_id(0)
    seqs = segr_ref.shape[0]
    tok = hid_ref.shape[0]

    @pl.when(step == 0)
    def _():
        for t in range(0, tok, HALF):
            x = hid_ref[t:t + HALF, :].astype(F32).T
            scale = lax.rsqrt(jnp.mean(x * x, axis=0, keepdims=True) + EPS)
            n1_ref[:, t:t + HALF] = (x * scale * column(gain1_ref)).astype(BF16)
        relt[...] = rel_ref[...].T
        lines[...] = jnp.zeros_like(lines)
        lines[:HEADS, :BUCKETS] = tab_ref[...]
        for s in range(seqs):
            line = segr_ref[s:s + 1, :]
            across = jnp.broadcast_to(line, (LEN, LEN))
            mask[s] = jnp.where(across.T == across, 0.0, -1000000000.0)

    for w_ref, o_ref in ((wq_ref, q_ref), (wk_ref, k_ref), (wv_ref, v_ref)):
        o_ref[...] = dot_tn(w_ref[...], n1_ref[...]).astype(BF16)

    @pl.loop(0, GROUP)
    def _(h):
        head = step * GROUP + h
        row = lines[pl.ds(head, 1), :]
        line = jnp.broadcast_to(row, (LEN, LANES))
        for c in range(0, LEN, LANES):
            bias[:, c:c + LANES] = jnp.take_along_axis(line, relt[:, c:c + LANES], axis=1)
        at = pl.ds(pl.multiple_of(h * HEAD_DIM, HEAD_DIM), HEAD_DIM)
        out_at = pl.ds(pl.multiple_of(head * HEAD_DIM, HEAD_DIM), HEAD_DIM)
        for s in range(seqs):
            key = k_ref[at, s * LEN:(s + 1) * LEN]
            value = v_ref[at, s * LEN:(s + 1) * LEN]
            for c in range(0, LEN, HALF):
                cols = slice(s * LEN + c, s * LEN + c + HALF)
                query = q_ref[at, cols] * jnp.asarray(HEAD_DIM ** -0.5, BF16)
                score = dot_tn(key, query) + bias[:, c:c + HALF] + mask[s, :, c:c + HALF]
                peak = jnp.max(score, axis=0, keepdims=True)
                weight = jnp.exp(score - peak)
                total = jnp.sum(weight, axis=0, keepdims=True)
                prob = (weight * (1.0 / total)).astype(BF16)
                p_ref[h, s, :, c:c + HALF] = prob
                attn_ref[out_at, cols] = dot_nn(value, prob).astype(BF16)

    @pl.when(step == pl.num_programs(0) - 1)
    def _():
        experts = route_ref.shape[0]
        for t in range(0, tok, HALF):
            cols = slice(t, t + HALF)
            x = hid_ref[t:t + HALF, :].astype(F32).T
            resid = x + dot_tn(wout_ref[...], attn_ref[:, cols])
            resid_ref[:, cols] = resid
            scale = lax.rsqrt(jnp.mean(resid * resid, axis=0, keepdims=True) + EPS)
            n2 = (resid * scale * column(gain2_ref)).astype(BF16)
            n2_ref[:, cols] = n2
            logits = dot_nn(wr_ref[...], n2)
            top = jnp.max(logits, axis=0, keepdims=True)
            e = jnp.exp(logits - top)
            route = e / jnp.sum(e, axis=0, keepdims=True)
            route_ref[:, cols] = route
            hot = lax.broadcasted_iota(jnp.int32, (experts, HALF), 0) == ids_ref[:, cols]
            gate_ref[:, cols] = jnp.sum(jnp.where(hot, route, 0.0), axis=0, keepdims=True)
        hot = lax.broadcasted_iota(jnp.int32, (experts, tok), 0) == ids_ref[...]
        gates = jnp.where(hot, gate_ref[...], 0.0)
        place = (
            lax.broadcasted_iota(jnp.int32, (LANES, tok), 0) == pos_ref[...]
        ).astype(F32).astype(BF16)
        parts = [dot_nt(part, place) for part in split3(gates)]
        which = lax.broadcasted_iota(jnp.int32, (experts, 8, LANES), 1)
        spread = [jnp.broadcast_to(part[:, None, :], which.shape) for part in parts]
        gpack_ref[...] = jnp.where(
            which == 0, spread[0],
            jnp.where(which == 1, spread[1], jnp.where(which == 2, spread[2], 0.0)),
        ).astype(BF16)
        rows = packed_ref.shape[0]

        @pl.loop(0, rows // HALF)
        def _(r):
            base = pl.multiple_of(r * HALF, HALF)
            table = (lax.broadcasted_iota(jnp.int32, (HALF, tok), 0) + base == slot_ref[...])
            packed_ref[pl.ds(base, HALF), :] = dot_nt(
                table.astype(F32).astype(BF16), n2_ref[...]
            ).astype(BF16)


def front(hidden, gain1, w_qkv, w_out, table, gain2, w_router, ids, slot, pos, seg, rel, rows):
    tok, width = hidden.shape
    experts = w_router.shape[0]
    seqs = seg.shape[0]
    wspec = lambda part: pl.BlockSpec((width, GW), lambda i: (0, part * GROUPS + i))
    qspec = pl.BlockSpec((GW, tok), lambda i: (i, 0))
    sd = jax.ShapeDtypeStruct
    outs = (
        sd((width, tok), BF16), sd((width, tok), BF16), sd((width, tok), BF16),
        sd((width, tok), BF16), sd((HEADS, seqs, LEN, LEN), BF16), sd((width, tok), BF16),
        sd((width, tok), F32), sd((width, tok), BF16), sd((experts, tok), F32), sd((1, tok), F32),
        sd((rows, width), BF16), sd((experts, 8, LANES), BF16),
    )
    return pl.pallas_call(
        front_kernel,
        grid=(GROUPS,),
        in_specs=[
            whole((tok, width)), whole((1, width)), wspec(0), wspec(1), wspec(2),
            whole((width, width)), whole((HEADS, BUCKETS)), whole((1, width)),
            whole((experts, width)), whole((1, tok)), whole((1, tok)), whole((1, tok)),
            whole((seqs, LEN)), whole((LEN, LEN)),
        ],
        out_specs=(
            whole((width, tok)), qspec, qspec, qspec,
            pl.BlockSpec((GROUP, seqs, LEN, LEN), lambda i: (i, 0, 0, 0)),
            whole((width, tok)), whole((width, tok)), whole((width, tok)),
            whole((experts, tok)), whole((1, tok)), whole((rows, width)),
            whole((experts, 8, LANES)),
        ),
        out_shape=outs,
        scratch_shapes=[
            pltpu.VMEM((LEN, LEN), jnp.int32),
            pltpu.VMEM((seqs, LEN, LEN), F32),
            pltpu.VMEM((LEN, LEN), F32),
            pltpu.VMEM((16, LANES), F32),
        ],
        compiler_params=pltpu.CompilerParams(vmem_limit_bytes=58 * MIB),
        cost_estimate=pl.CostEstimate(flops=50 * MICRO, bytes_accessed=30 * MIB, transcendentals=0),
        name="front",
    )(
        hidden, gain1.reshape(1, width), w_qkv, w_qkv, w_qkv, w_out, table,
        gain2.reshape(1, width), w_router, ids, slot, pos,
        seg, rel,
    )


def combine_kernel(rows_ref, slot_ref, gate_ref, resid_ref, out_ref):
    total = rows_ref.shape[0]
    cols = slot_ref.shape[1]
    table = lax.broadcasted_iota(jnp.int32, (total, cols), 0) == slot_ref[...]
    combined = dot_tn(rows_ref[...], table.astype(F32).astype(BF16))
    out_ref[...] = (resid_ref[...] + gate_ref[...] * combined).T.astype(BF16)


def combine(rows, slot, gate, resid):
    total, width = rows.shape
    tok = slot.shape[1]
    line = pl.BlockSpec((1, HALF), lambda i: (0, i))
    return pl.pallas_call(
        combine_kernel,
        grid=(tok // HALF,),
        in_specs=[
            whole((total, width)), line, line, pl.BlockSpec((width, HALF), lambda i: (0, i)),
        ],
        out_specs=pl.BlockSpec((HALF, width), lambda i: (i, 0)),
        out_shape=jax.ShapeDtypeStruct((tok, width), BF16),
        compiler_params=pltpu.CompilerParams(vmem_limit_bytes=40 * MIB),
        cost_estimate=pl.CostEstimate(flops=6 * MICRO, bytes_accessed=8 * MIB, transcendentals=0),
        name="combine",
    )(rows, slot, gate, resid)


CUBE = 0.044715
ROOT = 0.7978845608028654
FTILE = 768


def gelu_pair(x):
    square = x * x
    t = jnp.tanh(ROOT * (x + CUBE * (x * square)))
    half = 0.5 + 0.5 * t
    slope = half + (0.5 * x) * (1.0 - t * t) * (ROOT + (3.0 * CUBE * ROOT) * square)
    return x * half, slope


def device_of(index):
    wide = lax.axis_size("wide")
    return (index // wide, lax.rem(index, wide))


def expert_kernel(
    block,
    packed, gpack, grows, w_in, w_down,
    dx_out, out_got, rest_out, active_out, ginner_out, gs_out, x_out, gg_out,
    xbuf, gatebuf, gbuf, win, wdown, active, slope, ginner, gs, dx, outs, ggsend, ggbuf,
    x_send, x_recv, gate_send, gate_recv, gg_ssem, gg_rsem, o_send, o_recv, self_sem, load_sem, store_sem,
):
    count = lax.axis_size("narrow") * lax.axis_size("wide")
    me = lax.axis_index("narrow") * lax.axis_size("wide") + lax.axis_index("wide")
    blocks = count // block
    mine = me // block
    capp = packed.shape[1]
    rows = block * capp
    total = count * capp
    hidden = w_in.shape[1]
    mesh_id = pl.DeviceIdType.MESH

    def x_copy(target, source):
        return pltpu.make_async_remote_copy(
            src_ref=packed.at[target], dst_ref=xbuf.at[source], send_sem=x_send.at[target],
            recv_sem=x_recv.at[source], device_id=device_of(target), device_id_type=mesh_id,
        )

    def gate_copy(target, source):
        return pltpu.make_async_remote_copy(
            src_ref=gpack.at[target], dst_ref=gatebuf.at[source], send_sem=gate_send.at[target],
            recv_sem=gate_recv.at[source], device_id=device_of(target), device_id_type=mesh_id,
        )

    def gg_copy(target, source):
        return pltpu.make_async_remote_copy(
            src_ref=ggsend.at[target], dst_ref=ggbuf.at[source], send_sem=gg_ssem.at[target],
            recv_sem=gg_rsem.at[source], device_id=device_of(target), device_id_type=mesh_id,
        )

    ahead = blocks // 2
    inner = lax.rem(me, block)

    def out_copy(c, j):
        target = lax.rem(mine + c, blocks) * block + j
        return pltpu.make_async_remote_copy(
            src_ref=outs.at[c * block + j], dst_ref=out_got.at[c * block + inner],
            send_sem=o_send.at[c * block + j], recv_sem=o_recv.at[c * block + inner],
            device_id=device_of(target), device_id_type=mesh_id,
        )

    def out_wait(c, j):
        return pltpu.make_async_remote_copy(
            src_ref=outs.at[c * block + j], dst_ref=out_got.at[c * block + j],
            send_sem=o_send.at[c * block + j], recv_sem=o_recv.at[c * block + j],
            device_id=device_of(lax.rem(me + 1, count)), device_id_type=mesh_id,
        )

    barrier = pltpu.get_barrier_semaphore()

    @pl.loop(1, count)
    def _(s):
        pl.semaphore_signal(
            barrier, inc=1, device_id=device_of(lax.rem(me + s, count)), device_id_type=mesh_id
        )

    loads = [
        pltpu.make_async_copy(w_in, win, load_sem.at[0]),
        pltpu.make_async_copy(w_down, wdown, load_sem.at[1]),
        pltpu.make_async_copy(grows, gbuf, load_sem.at[2]),
    ]
    own = [
        pltpu.make_async_copy(packed.at[me], xbuf.at[me], self_sem.at[0]),
        pltpu.make_async_copy(gpack.at[me], gatebuf.at[me], self_sem.at[1]),
    ]
    for copy in own + loads:
        copy.start()
    pl.semaphore_wait(barrier, count - 1)

    @pl.loop(0, blocks)
    def _(c):
        there = lax.rem(mine + blocks - c, blocks)

        @pl.loop(0, block)
        def _(j):
            target = there * block + j

            @pl.when(target != me)
            def _():
                gate_copy(target, me).start()
                x_copy(target, me).start()

    for copy in own + loads:
        copy.wait()

    def stores(at):
        return [
            pltpu.make_async_copy(dx.at[at], dx_out.at[at], store_sem.at[0]),
            pltpu.make_async_copy(active.at[at], active_out.at[at], store_sem.at[1]),
            pltpu.make_async_copy(ginner.at[at], ginner_out.at[at], store_sem.at[2]),
            pltpu.make_async_copy(gs.at[at], gs_out.at[at], store_sem.at[3]),
        ]

    @pl.loop(0, blocks)
    def _(c):
        here = lax.rem(mine + c, blocks)
        first = here * block

        @pl.loop(0, block)
        def _(j):
            source = first + j

            @pl.when(source != me)
            def _():
                gate_copy(me, source).wait_recv()
                x_copy(me, source).wait_recv()

        at = pl.ds(pl.multiple_of(here * rows, rows), rows)
        group = pl.ds(first, block)
        x = xbuf[group].reshape(rows, xbuf.shape[2])

        @pl.loop(0, hidden // FTILE)
        def _(f):
            tile = pl.ds(pl.multiple_of(f * FTILE, FTILE), FTILE)
            value, grad = gelu_pair(dot_nn(x, win[:, tile]))
            active[at, tile] = value.astype(BF16)
            slope[:, tile] = grad

        result = dot_nn(active[at, :], wdown[...]).astype(BF16)
        outs[pl.ds(c * block, block)] = result.reshape(block, capp, result.shape[1])

        @pl.when(c < ahead)
        def _():
            @pl.loop(0, block)
            def _(j):
                @pl.when(first + j != me)
                def _():
                    out_copy(c, j).start()

        g = gbuf[group].astype(F32)
        diag = (
            lax.broadcasted_iota(jnp.int32, (block, capp, LANES), 1)
            == lax.broadcasted_iota(jnp.int32, (block, capp, LANES), 2)
        )
        gate = jnp.sum(gatebuf[group].astype(F32), axis=1)
        gate = jnp.sum(
            jnp.where(diag, gate[:, None, :], 0.0), axis=2, keepdims=True
        )
        gs[at, :] = (gate * g).astype(BF16).reshape(rows, g.shape[2])
        gg = jnp.sum(g * result.astype(F32).reshape(g.shape), axis=2, keepdims=True)
        gg = jnp.sum(jnp.where(diag, gg, 0.0), axis=1)
        which = lax.broadcasted_iota(jnp.int32, (block, 8, LANES), 1)
        high, mid, low = [part.astype(F32)[:, None, :] for part in split3(gg)]
        ggsend[group] = jnp.where(
            which == 0, high, jnp.where(which == 1, mid, jnp.where(which == 2, low, 0.0))
        ).astype(BF16)

        @pl.loop(0, block)
        def _(j):
            source = first + j

            @pl.when(source != me)
            def _():
                gg_copy(source, me).start()

        @pl.loop(0, hidden // FTILE)
        def _(f):
            tile = pl.ds(pl.multiple_of(f * FTILE, FTILE), FTILE)
            grad = dot_nt(gs[at, :], wdown[tile, :])
            ginner[at, tile] = (grad * slope[:, tile]).astype(BF16)

        dx[at, :] = dot_nt(ginner[at, :], win[...]).astype(BF16)

        for copy in stores(at):
            copy.start()

    for copy in stores(pl.ds(0, total)):
        copy.wait()
    keep = [
        pltpu.make_async_copy(xbuf, x_out, load_sem.at[0]),
        pltpu.make_async_copy(ggsend.at[me], ggbuf.at[me], self_sem.at[0]),
        pltpu.make_async_copy(outs.at[inner], out_got.at[inner], self_sem.at[1]),
        pltpu.make_async_copy(
            outs.at[pl.ds(ahead * block, count - ahead * block)], rest_out, load_sem.at[1]
        ),
    ]
    for copy in keep:
        copy.start()

    @pl.loop(0, count)
    def _(other):
        @pl.when(other != me)
        def _():
            x_copy(other, me).wait_send()
            gate_copy(other, me).wait_send()
            gg_copy(other, me).wait_send()
            gg_copy(me, other).wait_recv()

    @pl.loop(0, ahead * block)
    def _(i):
        @pl.when(i != inner)
        def _():
            out_wait(i // block, lax.rem(i, block)).wait_send()
            out_wait(i // block, lax.rem(i, block)).wait_recv()

    for copy in keep:
        copy.wait()
    last = pltpu.make_async_copy(ggbuf, gg_out, load_sem.at[1])
    last.start()
    last.wait()


def block_of(count, capp):
    block = 1
    while block * 4 <= count and block * 2 * capp <= 320:
        block *= 2
    return block


def expert(packed, gpack, grows, w_in, w_down):
    count, capp, width = packed.shape
    hidden = w_in.shape[1]
    block = block_of(count, capp)
    early = (count // block // 2) * block
    rows = block * capp
    total = count * capp
    sd = jax.ShapeDtypeStruct
    anyspec = pl.BlockSpec(memory_space=pl.ANY)
    dma = pltpu.SemaphoreType.DMA
    return pl.pallas_call(
        functools.partial(expert_kernel, block),
        in_specs=[anyspec] * 5,
        out_specs=(anyspec,) * 8,
        out_shape=(
            sd((total, width), BF16), sd((early, capp, width), BF16),
            sd((count - early, capp, width), BF16), sd((total, hidden), BF16), sd((total, hidden), BF16), sd((total, width), BF16), sd((count, capp, width), BF16),
            sd((count, 8, LANES), BF16),
        ),
        scratch_shapes=[
            pltpu.VMEM((count, capp, width), BF16), pltpu.VMEM((count, 8, LANES), BF16),
            pltpu.VMEM((count, capp, width), BF16), pltpu.VMEM((width, hidden), BF16),
            pltpu.VMEM((hidden, width), BF16), pltpu.VMEM((total, hidden), BF16),
            pltpu.VMEM((rows, hidden), F32), pltpu.VMEM((total, hidden), BF16),
            pltpu.VMEM((total, width), BF16), pltpu.VMEM((total, width), BF16),
            pltpu.VMEM((count, capp, width), BF16), pltpu.VMEM((count, 8, LANES), BF16),
            pltpu.VMEM((count, 8, LANES), BF16),
            dma((count,)), dma((count,)), dma((count,)), dma((count,)), dma((count,)), dma((count,)),
            dma((early,)), dma((early,)), dma((2,)), dma((3,)), dma((4,)),
        ],
        compiler_params=pltpu.CompilerParams(
            collective_id=0, has_side_effects=True, vmem_limit_bytes=62 * MIB
        ),
        cost_estimate=pl.CostEstimate(flops=60 * MICRO, bytes_accessed=60 * 1024 * 1024, transcendentals=0),
        name="expert",
    )(packed, gpack, grows, w_in, w_down)


def weights_kernel(active_ref, gs_ref, x_ref, ginner_ref, down_ref, in_ref, xt):
    @pl.when(pl.program_id(0) == 0)
    def _():
        total = x_ref.shape[0]
        for t in range(0, total, HALF):
            xt[:, t:t + HALF] = x_ref[t:t + HALF, :].T

    down_ref[0] = dot_tn(active_ref[...], gs_ref[...])
    in_ref[0] = dot_nn(xt[...], ginner_ref[...])


def weight_grads(active, gs, x, ginner):
    total, hidden = active.shape
    width = gs.shape[1]
    tile = HALF
    cols = pl.BlockSpec((total, tile), lambda i: (0, i))
    return pl.pallas_call(
        weights_kernel,
        grid=(hidden // tile,),
        in_specs=[cols, whole((total, width)), whole((total, width)), cols],
        out_specs=(
            pl.BlockSpec((1, tile, width), lambda i: (0, i, 0)),
            pl.BlockSpec((1, width, tile), lambda i: (0, 0, i)),
        ),
        out_shape=(
            jax.ShapeDtypeStruct((1, hidden, width), F32),
            jax.ShapeDtypeStruct((1, width, hidden), F32),
        ),
        scratch_shapes=[pltpu.VMEM((width, total), BF16)],
        compiler_params=pltpu.CompilerParams(vmem_limit_bytes=62 * MIB),
        cost_estimate=pl.CostEstimate(flops=18 * MICRO, bytes_accessed=36 * 1024 * 1024, transcendentals=0),
        name="weight_grads",
    )(active, gs, x, ginner)
PIECES = 32
BIG = 2
UNITS = BIG + GROUPS
TROWS = 16
LATE = 24
LAST_PHASE = 7


def norm_back(grad, source, gain):
    scale = lax.rsqrt(jnp.mean(source * source, axis=0, keepdims=True) + EPS)
    normed = source * scale
    scaled = grad * gain
    inner = jnp.mean(scaled * normed, axis=0, keepdims=True)
    part = grad * normed
    part = part[:, :LANES] + part[:, LANES:]
    return scale * (scaled - normed * inner), part


def back_kernel(
    block,
    dx_ref, gg_ref, slot_ref, pos_ref, ids_ref, route_ref, gate_ref, n2_ref, attn_ref,
    gain1_ref, gain2_ref, wr_ref, wout_ref, resid_any, g_any, hid_any, n1_any, q_any, k_any, v_any, p_any,
    wqkv_any, rel_any, rest_any,
    ingrad_any, out_got, big_out, small_out, early_out, late_out,
    gres, ga, gn1, dv, soft, hid_ref, n1_ref, q_ref, k_ref, v_ref, wqkv_ref, rel_ref, acc,
    *buffers_and_rest,
):
    buffers = buffers_and_rest[:16]
    inside = buffers[7].shape == big_out.shape
    big = buffers[:7] + (buffers[7] if inside else big_out,)
    small = buffers[8:15] + (buffers[15] if inside else small_out,)
    (
        early, early_got, late, late_got, send, recv, xsend, xrecv, esend, erecv, lsend, lrecv, osend, orecv, load_sem, store_sem, stage_sem, write_sem,
    ) = buffers_and_rest[16:]
    dq, dk = dv.at[pl.ds(0, GW)], dv.at[pl.ds(GW, GW)]
    step = pl.program_id(0)
    pair = pl.program_id(1)
    tok = g_any.shape[0]
    seqs = tok // LEN
    experts = route_ref.shape[0]
    total = dx_ref.shape[0]
    width = g_any.shape[1]
    narrow_n, wide_n = lax.axis_size("narrow"), lax.axis_size("wide")
    n, w = lax.axis_index("narrow"), lax.axis_index("wide")
    core, zed = lax.rem(w, 2), lax.rem(w // 2, 4)
    ex, why = lax.rem(n, 2), lax.rem(n // 2, 2)
    more_n = (narrow_n // 4) * (wide_n // 8)
    more_w = wide_n // 8
    more = (n // 4) * more_w + w // 8
    mesh_id = pl.DeviceIdType.MESH
    core_dev = (n, w + 1 - 2 * core)
    ex_dev = (n + 1 - 2 * ex, w)
    why_dev = (n + 2 - 4 * why, w)

    def zed_dev(step):
        return (n, w + 2 * (lax.rem(zed + step, 4) - zed))

    def more_dev(step):
        other = lax.rem(more + step, more_n)
        return (n + 4 * (other // more_w - more // more_w),
                w + 8 * (lax.rem(other, more_w) - lax.rem(more, more_w)))

    def unit(u):
        if isinstance(u, int):
            return (big, u, u) if u < BIG else (small, u - BIG, u)
        return small, u, u + BIG

    def ref(which, u):
        group, at, _ = unit(u)
        return group[which], at

    def view(which, u, *more):
        group, at, _ = unit(u)
        return group[which].at[(at,) + more]

    def land(u, q, at):
        return view(7, u, q, at)

    def spot(q):
        first, second = (ex, why) if q == 0 else (why, ex)
        b16 = core * 16
        b8 = b16 + first * 8
        b4 = b8 + second * 4
        return first, second, b16, b8, b4

    def remote(src, dst, k, u, q, dev):
        return pltpu.make_async_remote_copy(
            src_ref=src, dst_ref=dst, send_sem=send.at[k, unit(u)[2], q], recv_sem=recv.at[k, unit(u)[2], q],
            device_id=dev, device_id_type=mesh_id,
        )

    def outgoing(phase, u, q):
        first, second, b16, b8, b4 = spot(q)
        one, two = (ex_dev, why_dev) if q == 0 else (why_dev, ex_dev)
        if phase == 0:
            return [remote(view(0, u, q, pl.ds(16 - b16, 16)), view(2, u, q), 0, u, q, core_dev)]
        if phase == 1:
            src = view(0, u, q, pl.ds(b16 + (1 - first) * 8, 8))
            return [remote(src, view(3, u, q), 1, u, q, one)]
        if phase == 2:
            src = view(0, u, q, pl.ds(b8 + (1 - second) * 4, 4))
            return [remote(src, view(4, u, q), 2, u, q, two)]
        if phase == 3:
            return [
                remote(view(0, u, q, b4 + lax.rem(zed + step, 4)), view(5, u, q, step - 1),
                       2 + step, u, q, zed_dev(step))
                for step in (1, 2, 3)
            ]
        if phase == 4:
            mine = land(u, q, b4 + zed)
            return [remote(view(1, u, q), mine, 5 + step, u, q, zed_dev(step)) for step in (1, 2, 3)]
        if phase == 5:
            mine = land(u, q, pl.ds(b4, 4))
            return [remote(mine, mine, 9, u, q, two)]
        if phase == 6:
            mine = land(u, q, pl.ds(b8, 8))
            return [remote(mine, mine, 10, u, q, one)]
        mine = land(u, q, pl.ds(b16, 16))
        return [remote(mine, mine, 11, u, q, core_dev)]

    def incoming(phase, u, q):
        first, second, b16, b8, b4 = spot(q)
        if phase < 4:
            return outgoing(phase, u, q)
        if phase == 4:
            return [
                remote(view(1, u, q), land(u, q, b4 + lax.rem(zed + 4 - step, 4)),
                       5 + step, u, q, zed_dev(step))
                for step in (1, 2, 3)
            ]
        if phase == 5:
            there = land(u, q, pl.ds(b8 + (1 - second) * 4, 4))
            return [remote(there, there, 9, u, q, core_dev)]
        if phase == 6:
            there = land(u, q, pl.ds(b16 + (1 - first) * 8, 8))
            return [remote(there, there, 10, u, q, core_dev)]
        there = land(u, q, pl.ds(16 - b16, 16))
        return [remote(there, there, 11, u, q, core_dev)]

    def add(u, q, start, count, which):
        own, at = ref(0, u)
        got = ref(which, u)[0]

        @pl.loop(0, count)
        def _(i):
            own[at, q, start + i] = (
                own[at, q, start + i].astype(F32) + got[at, q, i].astype(F32)
            ).astype(BF16)

    def spread(u, q):
        (done, at), (extra, _) = ref(1, u), ref(6, u)
        extra[at, q, more] = done[at, q]
        copies = [
            pltpu.make_async_remote_copy(
                src_ref=view(6, u, q, more), dst_ref=view(6, u, q, more),
                send_sem=xsend.at[unit(u)[2], q, step], recv_sem=xrecv.at[unit(u)[2], q, step],
                device_id=more_dev(step), device_id_type=mesh_id,
            )
            for step in range(1, more_n)
        ]
        for copy in copies:
            copy.start()
        for step in range(1, more_n):
            other = lax.rem(more + more_n - step, more_n)
            pltpu.make_async_remote_copy(
                src_ref=view(6, u, q, more), dst_ref=view(6, u, q, other),
                send_sem=xsend.at[unit(u)[2], q, step], recv_sem=xrecv.at[unit(u)[2], q, step],
                device_id=more_dev(step), device_id_type=mesh_id,
            ).wait_recv()
        for copy in copies:
            copy.wait_send()
        total = extra[at, q, 0].astype(F32)
        for i in range(1, more_n):
            total = total + extra[at, q, i].astype(F32)
        done[at, q] = total.astype(BF16)

    def keep(u, q):
        at = spot(q)[4] + zed
        return pltpu.make_async_copy(view(1, u, q), land(u, q, at), store_sem.at[unit(u)[2], q])

    def settle(phase, u, q):
        first, second, b16, b8, b4 = spot(q)
        if phase == 0:
            add(u, q, b16, 16, 2)
        elif phase == 1:
            add(u, q, b8, 8, 3)
        elif phase == 2:
            add(u, q, b4, 4, 4)
        elif phase == 3:
            (own, at), (done, _), (got, _) = ref(0, u), ref(1, u), ref(5, u)
            done[at, q] = (
                own[at, q, b4 + zed].astype(F32) + got[at, q, 0].astype(F32)
                + (got[at, q, 1].astype(F32) + got[at, q, 2].astype(F32))
            ).astype(BF16)
            if more_n > 1:
                spread(u, q)
            keep(u, q).start()
        elif phase == 4:
            keep(u, q).wait()

    bits = []
    for axis, count in (("wide", wide_n), ("narrow", narrow_n)):
        size = 1
        while size < count:
            at = lax.rem((w if axis == "wide" else n) // size, 2)
            move = size - 2 * size * at
            bits.append((n, w + move) if axis == "wide" else (n + move, w))
            size *= 2
    levels = len(bits)
    early_levels = early_got.shape[0] if early.shape[0] > 1 else 0

    def swap(level, mine, got, ssem, rsem):
        return pltpu.make_async_remote_copy(
            src_ref=mine.at[level], dst_ref=got.at[level], send_sem=ssem.at[level],
            recv_sem=rsem.at[level], device_id=bits[level], device_id_type=mesh_id,
        )

    def climb(level, mine, got, ssem, rsem):
        copy = swap(level, mine, got, ssem, rsem)
        copy.wait_recv()
        copy.wait_send()
        mine[level + 1] = mine[level] + got[level]
        if level + 1 < levels:
            swap(level + 1, mine, got, ssem, rsem).start()

    def climb_early(level):
        climb(level, early, early_got, esend, erecv)

    def climb_late(level):
        climb(level, late, late_got, lsend, lrecv)

    count = narrow_n * wide_n
    blocks = count // block
    ahead = blocks // 2
    index = n * wide_n + w
    rest = rest_any.shape[0]

    def out_copy(i):
        target = lax.rem(index // block + ahead + i // block, blocks) * block + lax.rem(i, block)
        return pltpu.make_async_remote_copy(
            src_ref=rest_any.at[i],
            dst_ref=out_got.at[(i // block) * block + lax.rem(index, block)],
            send_sem=osend.at[i], recv_sem=orecv.at[(i // block) * block + lax.rem(index, block)],
            device_id=device_of(target), device_id_type=mesh_id,
        )

    def out_wait(i):
        return pltpu.make_async_remote_copy(
            src_ref=rest_any.at[i], dst_ref=out_got.at[i], send_sem=osend.at[i],
            recv_sem=orecv.at[i], device_id=core_dev, device_id_type=mesh_id,
        )

    def begin(u):
        for q in range(2):
            for copy in outgoing(0, u, q):
                copy.start()

    def advance(u, phase):
        for q in range(2):
            for copy in incoming(phase, u, q):
                copy.wait_recv()
            for copy in outgoing(phase, u, q):
                copy.wait_send()
            settle(phase, u, q)
            if phase < LAST_PHASE:
                for copy in outgoing(phase + 1, u, q):
                    copy.start()
        if inside and phase == LAST_PHASE:
            write_out(u).start()

    def write_out(u):
        group, at, flat = unit(u)
        out = big_out if u < BIG else small_out
        return pltpu.make_async_copy(group[7].at[at], out.at[at], write_sem.at[flat])

    def place(u, first, value):
        own, at = ref(0, u)
        half = own.shape[4]
        count = value.shape[1]
        blocks = value.reshape(PIECES, width // PIECES, count).astype(BF16)
        done = 0
        while done < count:
            q, within = (first + done) // half, (first + done) % half
            size = min(half - within, count - done)
            own[at, q, :, :, within:within + size] = blocks[:, :, done:done + size]
            done += size

    def soft_load(group):
        at = pl.ds(group * GROUP, GROUP)
        return pltpu.make_async_copy(p_any.at[at], soft.at[at], load_sem.at[group])

    pairs = ((n1_any, n1_ref), (wqkv_any, wqkv_ref), (v_any, v_ref), (k_any, k_ref), (q_any, q_ref),
             (rel_any, rel_ref))
    loads = [
        pltpu.make_async_copy(src, dst, load_sem.at[GROUPS + i]) for i, (src, dst) in enumerate(pairs)
    ]

    rows_load = [
        pltpu.make_async_copy(src, hid_ref, load_sem.at[GROUPS + 6 + i])
        for i, src in enumerate((g_any, hid_any))
    ]

    barrier = pltpu.get_barrier_semaphore()
    greet = [core_dev, ex_dev, why_dev] + [zed_dev(move) for move in (1, 2, 3)]
    greet += [more_dev(move) for move in range(1, more_n)] + bits

    @pl.when((step == 0) & (pair == 0))
    def _():
        first = pltpu.make_async_copy(resid_any, gres, stage_sem)
        first.start()
        rows_load[0].start()
        for group in range(GROUPS):
            soft_load(group).start()
        for copy in loads:
            copy.start()
        for dev in greet:
            pl.semaphore_signal(barrier, inc=1, device_id=dev, device_id_type=mesh_id)

        @pl.loop(0, rest)
        def _(i):
            source = lax.rem(
                index // block + 2 * blocks - ahead - i // block, blocks
            ) * block + lax.rem(i, block)
            pl.semaphore_signal(
                barrier, inc=1, device_id=device_of(source), device_id_type=mesh_id
            )

        pl.semaphore_wait(barrier, len(greet) + rest)

        @pl.loop(0, rest)
        def _(i):
            out_copy(i).start()

        hot = lax.broadcasted_iota(jnp.int32, (experts, tok), 0) == ids_ref[...]
        where = (
            lax.broadcasted_iota(jnp.int32, (LANES, tok), 0) == pos_ref[...]
        ).astype(F32).astype(BF16)
        grad_gate = jnp.zeros((1, tok), F32)
        for e in range(0, experts, 32):
            found = dot_nn(gg_ref[e:e + 32].reshape(256, LANES), where)
            found = jnp.sum(found.reshape(32, 8, tok), axis=1)
            grad_gate += jnp.sum(jnp.where(hot[e:e + 32], found, 0.0), axis=0, keepdims=True)
        first.wait()
        rows_load[0].wait()
        grad_logits = (
            (grad_gate * gate_ref[...]) * (hot.astype(F32) - route_ref[...])
        ).astype(BF16)
        early[0, :experts, :] = dot_nt(grad_logits, n2_ref[...])
        gain_grad = jnp.zeros((width, LANES), F32)
        for t in range(0, tok, HALF):
            cols = slice(t, t + HALF)
            gn2 = dot_tn(wr_ref[...], grad_logits[:, cols])
            size = total if total <= 1280 else 512
            for r in range(0, total, size):
                table = lax.broadcasted_iota(jnp.int32, (size, HALF), 0) + r == slot_ref[:, cols]
                gn2 = gn2 + dot_tn(dx_ref[r:r + size, :], table.astype(F32).astype(BF16))
            branch, part = norm_back(gn2, gres[:, cols], column(gain2_ref))
            gain_grad = gain_grad + part
            gr = hid_ref[t:t + HALF, :].astype(F32).T + branch
            gres[:, cols] = gr
            ga[:, cols] = gr.astype(BF16)
        early[0, experts:, :] = jnp.broadcast_to(
            jnp.sum(gain_grad.T, axis=0, keepdims=True), (8, width)
        )
        for c in range(0, width, HALF):
            place(0, c, dot_nt(attn_ref[...], ga[c:c + HALF, :]))
        rows_load[1].start()
        begin(0)
        if early_levels:
            swap(0, early, early_got, esend, erecv).start()
        for t in range(0, tok, HALF):
            cols = slice(t, t + HALF)
            ga[:, cols] = dot_nn(wout_ref[...], ga[:, cols]).astype(BF16)
        for group in range(GROUPS):
            soft_load(group).wait()

            @pl.loop(group * GROUP, (group + 1) * GROUP)
            def _(head):
                at = pl.ds(pl.multiple_of(head * HEAD_DIM, HEAD_DIM), HEAD_DIM)
                for s in range(seqs):
                    row = slice(s * LEN, (s + 1) * LEN)
                    dv[at, row] = dot_nt(ga[at, row], soft[head, s]).astype(BF16)

        loads[0].wait()
        for c in range(0, width, GW):
            place(1, c, dot_nt(n1_ref[...], dv[c:c + GW, :]))
        begin(1)
        loads[1].wait()
        for t in range(0, tok, HALF):
            gn1[:, t:t + HALF] = dot_nn(wqkv_ref[:, 2 * width:], dv[:, t:t + HALF])
        for copy in loads[2:5]:
            copy.wait()

    @pl.loop(0, PAIR)
    def _(h):
        turn = pair * PAIR + h
        head = step * GROUP + turn
        at = pl.ds(pl.multiple_of(turn * HEAD_DIM, HEAD_DIM), HEAD_DIM)
        all_at = pl.ds(pl.multiple_of(head * HEAD_DIM, HEAD_DIM), HEAD_DIM)
        for s in range(seqs):
            row = slice(s * LEN, (s + 1) * LEN)
            value = v_ref[all_at, row]
            for c in range(0, LEN, HALF):
                cols = slice(s * LEN + c, s * LEN + c + HALF)
                grad = ga[all_at, cols]
                inner = jnp.sum(
                    grad.astype(F32) * attn_ref[all_at, cols].astype(F32), axis=0, keepdims=True
                )
                gp = dot_tn(value, grad)
                soft[head, s, :, c:c + HALF] = (
                    soft[head, s, :, c:c + HALF].astype(F32) * (gp - inner)
                ).astype(BF16)
            ds = soft[head, s]
            factor = HEAD_DIM ** -0.5
            dq[at, row] = (dot_nn(k_ref[all_at, row], ds) * factor).astype(BF16)
            dk[at, row] = (dot_nt(q_ref[all_at, row], ds) * factor).astype(BF16)

        for number in range(HEADS):
            todo = [(u, phase) for u, phase, at_head in SCHEDULE if at_head == number]
            rise = [level for level, at_head in enumerate(EARLY_LEVELS)
                    if at_head == number and level < early_levels]
            if todo or rise:
                @pl.when(head == number)
                def _():
                    for u, phase in todo:
                        advance(u, phase)
                    for level in rise:
                        climb_early(level)

    @pl.when(pair == pl.num_programs(1) - 1)
    def _():
        for part, d in enumerate((dq, dk)):
            place(step, part * GW, dot_nt(n1_ref[...], d[...]))
        begin(step)
        for part, d in enumerate((dq, dk)):
            cols = pl.ds(pl.multiple_of(part * width + step * GW, GW), GW)
            gn1[...] += dot_nn(wqkv_ref[:, cols], d[...])

    @pl.when((step == pl.num_programs(0) - 1) & (pair == pl.num_programs(1) - 1))
    def _():
        planned = {(u, phase) for u, phase, at_head in SCHEDULE}
        left = {u: [phase for phase in range(LAST_PHASE + 1) if (u, phase) not in planned]
                for u in range(UNITS)}

        def push():
            for u in range(UNITS):
                if left[u]:
                    advance(u, left[u].pop(0))

        rows_load[1].wait()
        loads[5].wait()
        gain_grad = jnp.zeros((width, LANES), F32)
        for t in range(0, tok, HALF):
            cols = slice(t, t + HALF)
            x = hid_ref[t:t + HALF, :].astype(F32).T
            branch, part = norm_back(gn1[:, cols], x, column(gain1_ref))
            gain_grad = gain_grad + part
            gres[:, cols] = gres[:, cols] + branch
            if t == HALF:
                push()
        pltpu.make_async_copy(gres, ingrad_any, stage_sem).start()
        line = jnp.sum(gain_grad.T, axis=0, keepdims=True)
        late[0] = jnp.zeros((LATE, LANES), F32)
        for i in range(width // LANES):
            late[0, i:i + 1, :] = line[:, i * LANES:(i + 1) * LANES]
        push()
        lines = HEADS * seqs
        acc[...] = jnp.zeros_like(acc)
        chunks = 2
        for chunk in range(chunks):
            @pl.loop(chunk * (LEN // TROWS // chunks), (chunk + 1) * (LEN // TROWS // chunks))
            def _(r):
                base = pl.multiple_of(r * TROWS, TROWS)
                lhs = soft[:, :, pl.ds(base, TROWS), :].reshape(lines * TROWS, LEN)
                rel = rel_ref[pl.ds(base, TROWS), :]
                hot = (
                    rel[:, None, :]
                    == lax.broadcasted_iota(jnp.int32, (TROWS, BUCKETS, LEN), 1)
                ).astype(F32).astype(BF16).reshape(TROWS * BUCKETS, LEN)
                acc[...] += dot_nt(lhs, hot)

            push()
        rows = lax.broadcasted_iota(jnp.int32, acc.shape, 0) % TROWS
        cols = lax.broadcasted_iota(jnp.int32, acc.shape, 1) // BUCKETS
        kept = jnp.where(rows == cols, acc[...], 0.0)
        per_head = jnp.sum(kept.reshape(HEADS, seqs * TROWS, acc.shape[1]), axis=1)
        fold = (
            lax.broadcasted_iota(jnp.int32, (LANES, acc.shape[1]), 1) % BUCKETS
            == lax.broadcasted_iota(jnp.int32, (LANES, acc.shape[1]), 0)
        ).astype(F32)
        late[0, 8:8 + HEADS, :] = lax.dot_general(
            per_head, fold, (((1,), (1,)), ((), ())), precision=lax.Precision.HIGHEST,
            preferred_element_type=F32,
        )
        swap(0, late, late_got, lsend, lrecv).start()
        level = 0
        while any(left.values()) or level < levels:
            push()
            if level < levels:
                climb_late(level)
                level += 1
        for level in range(early_levels):
            if level >= len(EARLY_LEVELS):
                climb_early(level)
        pltpu.make_async_copy(gres, ingrad_any, stage_sem).wait()

        @pl.loop(0, rest)
        def _(i):
            out_wait(i).wait_send()
            out_wait(i).wait_recv()

        if inside:
            for u in range(UNITS):
                write_out(u).wait()
        early_out[...] = early[early_levels]
        late_out[...] = late[levels]


EARLY_MOST = 64
EARLY_LEVELS = (1, 3, 5, 7, 9)
SCHEDULE = (
    [(0, phase, at) for phase, at in enumerate((0, 2, 4, 6, 8, 10))]
    + [(1, phase, at) for phase, at in enumerate((1, 3, 5, 8, 11))]
    + [(2, phase, at) for phase, at in enumerate((5, 7, 10))]
    + [(3, phase, at) for phase, at in enumerate((9, 11))]
)


def back(dx, gg, slot, pos, ids, route, gate, resid, n2, attn, g, hidden, n1, q, k, v, p, gain1, gain2,
         w_router, w_out, w_qkv, relt, rest, block):
    tok, width = hidden.shape
    experts = w_router.shape[0]
    total = dx.shape[0]
    seqs = p.shape[1]
    narrow_n, wide_n = lax.axis_size("narrow"), lax.axis_size("wide")
    levels = (narrow_n * wide_n).bit_length() - 1
    more_n = (narrow_n // 4) * (wide_n // 8)
    early_levels = levels if experts <= EARLY_MOST else 0
    rows = width // PIECES
    anyspec = pl.BlockSpec(memory_space=pl.ANY)
    sd = jax.ShapeDtypeStruct
    dma = pltpu.SemaphoreType.DMA
    vm = pltpu.VMEM

    def bufs(number, half):
        return [
            vm((number, 2) + lead + (rows, half), BF16)
            for lead in ((PIECES,), (), (16,), (8,), (4,), (3,), (more_n,))
        ] + [vm((number, 2, PIECES, rows, half) if more_n == 1 else (8, LANES), BF16)]

    return pl.pallas_call(
        functools.partial(back_kernel, block),
        grid=(GROUPS, GROUP // PAIR),
        in_specs=[
            whole((total, width)), whole((experts, 8, LANES)), whole((1, tok)), whole((1, tok)),
            whole((1, tok)), whole((experts, tok)), whole((1, tok)), whole((width, tok)),
            whole((width, tok)), whole((1, width)), whole((1, width)),
            whole((experts, width)), whole((width, width)),
        ] + [anyspec] * 11,
        out_specs=(
            anyspec, anyspec, anyspec, anyspec, whole((experts + 8, width)), whole((LATE, LANES)),
        ),
        out_shape=(
            sd((width, tok), F32), sd(rest.shape, BF16), sd((BIG, 2, PIECES, rows, width // 2), BF16),
            sd((GROUPS, 2, PIECES, rows, GW), BF16),
            sd((experts + 8, width), F32), sd((LATE, LANES), F32),
        ),
        scratch_shapes=[
            vm((width, tok), F32), vm((width, tok), BF16), vm((width, tok), F32),
            vm((width, tok), BF16),
            vm((HEADS, seqs, LEN, LEN), BF16), vm((tok, width), BF16), vm((width, tok), BF16),
            vm((width, tok), BF16), vm((width, tok), BF16), vm((width, tok), BF16),
            vm(w_qkv.shape, BF16), vm((LEN, LEN), jnp.int32), vm((HEADS * seqs * TROWS, TROWS * BUCKETS), F32),
            *bufs(BIG, width // 2), *bufs(GROUPS, GW),
            vm((early_levels + 1, experts + 8, width), F32),
            vm((max(early_levels, 1), experts + 8, width) if early_levels else (1, 8, width), F32),
            vm((levels + 1, LATE, LANES), F32), vm((levels, LATE, LANES), F32),
            dma((12, UNITS, 2)), dma((12, UNITS, 2)), dma((UNITS, 2, more_n)),
            dma((UNITS, 2, more_n)), dma((levels,)), dma((levels,)), dma((levels,)), dma((levels,)),
            dma((rest.shape[0],)), dma((rest.shape[0],)),
            dma((GROUPS + 8,)), dma((UNITS, 2)), dma(()), dma((UNITS,)),
        ],
        compiler_params=pltpu.CompilerParams(
            collective_id=1, has_side_effects=True, vmem_limit_bytes=63 * MIB
        ),
        cost_estimate=pl.CostEstimate(flops=80 * MICRO, bytes_accessed=50 * MIB, transcendentals=0),
        name="back",
    )(
        dx, gg, slot, pos, ids, route, gate, n2, attn, gain1.reshape(1, width),
        gain2.reshape(1, width), w_router, w_out, resid, g, hidden, n1, q, k, v, p, w_qkv, relt, rest,
    )


def finish_kernel(
    early_ref, late_ref, slot_ref, gate_ref, resid_ref, big_ref, small_ref, grad_ref,
    router_ref, tail_ref,
    out_ref, qkv_ref, proj_ref, ingrad_ref, gain1_ref, gain2_ref, table_ref, routerg_ref,
):

    @pl.when(pl.program_id(0) == 0)
    def _():
        experts = routerg_ref.shape[0]
        for i in range(gain1_ref.shape[0] // LANES):
            gain1_ref[i * LANES:(i + 1) * LANES] = tail_ref[i, :]
        gain2_ref[...] = router_ref[experts, :]
        table_ref[...] = tail_ref[8:8 + HEADS, :BUCKETS]
        routerg_ref[...] = router_ref[:experts, :]

    ingrad_ref[...] = grad_ref[...].T
    rows_a = early_ref.shape[0]
    cols = slot_ref.shape[1]
    combined = None
    for base, ref in ((0, early_ref), (rows_a, late_ref)):
        table = (
            lax.broadcasted_iota(jnp.int32, (ref.shape[0], cols), 0) + base == slot_ref[...]
        )
        part = dot_tn(ref[...], table.astype(F32).astype(BF16))
        combined = part if combined is None else combined + part
    out_ref[...] = (resid_ref[...] + gate_ref[...] * combined).T.astype(BF16)
    rows = qkv_ref.shape[0]
    half = big_ref.shape[4]
    width = 2 * half
    for q in range(2):
        proj_ref[:, q * half:(q + 1) * half] = big_ref[0, q].astype(F32).reshape(rows, half)
        start = 2 * width + q * half
        qkv_ref[:, start:start + half] = big_ref[1, q].astype(F32).reshape(rows, half)
        for group in range(GROUPS):
            start = q * width + group * GW
            qkv_ref[:, start:start + GW] = small_ref[group, q].astype(F32).reshape(rows, GW)


def finish(out_a, out_b, slot, gate, resid, big, small, grad, router, tail):
    tok = slot.shape[1]
    width = resid.shape[0]
    steps = tok // HALF
    line = pl.BlockSpec((1, HALF), lambda i: (0, i))
    pieces = big.shape[2] // steps
    rows = width // steps
    return pl.pallas_call(
        finish_kernel,
        grid=(steps,),
        in_specs=[
            whole(out_a.shape), whole(out_b.shape), line, line,
            pl.BlockSpec((width, HALF), lambda i: (0, i)),
            pl.BlockSpec(big.shape[:2] + (pieces,) + big.shape[3:], lambda i: (0, 0, i, 0, 0)),
            pl.BlockSpec(small.shape[:2] + (pieces,) + small.shape[3:], lambda i: (0, 0, i, 0, 0)),
            pl.BlockSpec((width, HALF), lambda i: (0, i)), whole(router.shape), whole(tail.shape),
        ],
        out_specs=(
            pl.BlockSpec((HALF, width), lambda i: (i, 0)),
            pl.BlockSpec((rows, 3 * width), lambda i: (i, 0)),
            pl.BlockSpec((rows, width), lambda i: (i, 0)),
            pl.BlockSpec((HALF, width), lambda i: (i, 0)), whole((width,)), whole((width,)),
            whole((HEADS, BUCKETS)), whole((router.shape[0] - 8, width)),
        ),
        out_shape=(
            jax.ShapeDtypeStruct((tok, width), BF16),
            jax.ShapeDtypeStruct((width, 3 * width), F32),
            jax.ShapeDtypeStruct((width, width), F32),
            jax.ShapeDtypeStruct((tok, width), F32), jax.ShapeDtypeStruct((width,), F32),
            jax.ShapeDtypeStruct((width,), F32), jax.ShapeDtypeStruct((HEADS, BUCKETS), F32),
            jax.ShapeDtypeStruct((router.shape[0] - 8, width), F32),
        ),
        compiler_params=pltpu.CompilerParams(vmem_limit_bytes=62 * MIB),
        cost_estimate=pl.CostEstimate(flops=8 * MICRO, bytes_accessed=20 * MIB, transcendentals=0),
        name="finish",
    )(out_a, out_b, slot, gate, resid, big, small, grad, router, tail)


def matmul(a, b):
    return jnp.dot(a, b, preferred_element_type=F32)


AXES = ("narrow", "wide")


def exchange(v):
    return lax.all_to_all(v, AXES, split_axis=0, concat_axis=0, tiled=True)


def local(
    hidden_in, norm_gain_one, w_qkv, w_out, pos_table, norm_gain_two, w_router, w_in, w_down,
    expert_ids, segment_ids, rel_buckets, out_grad,
):
    experts = lax.axis_size("narrow") * lax.axis_size("wide")
    tok, width = hidden_in.shape
    w_router = w_router.T
    cap = max(2, (5 * tok + 4 * experts - 1) // (4 * experts))
    capp = (cap + 7) // 8 * 8
    rows = experts * capp
    ids = expert_ids.reshape(1, tok)
    slot, pos, g_packed = make_slots(experts, cap, capp, ids, out_grad)
    g_rows = exchange(g_packed.reshape(experts, capp, width))
    (n1, q, k, v, p, attn, resid, n2, route, gate, packed, gpack) = front(
        hidden_in, norm_gain_one, w_qkv, w_out, pos_table.T, norm_gain_two, w_router, ids, slot, pos,
        segment_ids, rel_buckets, rows,
    )
    block = block_of(experts, capp)
    dx, out_a, rest, active, ginner, gs, expert_in, gg = expert(
        packed.reshape(experts, capp, width), gpack, g_rows, w_in[0], w_down[0]
    )
    dx = exchange(dx.reshape(experts, capp, width)).reshape(rows, width)
    grad_w_down, grad_w_in = weight_grads(active, gs, expert_in.reshape(rows, width), ginner)
    dx, grad_w_down, grad_w_in = lax.optimization_barrier((dx, grad_w_down, grad_w_in))
    grad, out_b, big, small, early, late = back(
        dx, gg, slot, pos, ids, route, gate, resid, n2, attn, out_grad, hidden_in, n1, q, k, v, p,
        norm_gain_one, norm_gain_two, w_router, w_out, w_qkv, rel_buckets.T, rest, block,
    )
    if experts > EARLY_MOST:
        early = lax.psum(early, AXES)
    blocks = experts // block
    index = lax.axis_index("narrow") * lax.axis_size("wide") + lax.axis_index("wide")
    turn = lax.rem(index // block + blocks - ids // block, blocks)
    place = jnp.where(pos >= 0, (turn * block + lax.rem(ids, block)) * capp + pos, -1)
    layer_out, qkv_grad, out_grad_w, in_grad, gain1g, gain2g, tableg, routerg = finish(
        out_a.reshape(-1, width), out_b.reshape(-1, width), place, gate, resid, big, small, grad,
        early, late,
    )
    return (
        layer_out, in_grad, gain1g, qkv_grad, out_grad_w, tableg.T,
        gain2g, routerg.T, grad_w_in, grad_w_down,
    )


def solution(mesh):
    split = P(AXES, None)
    cube = P(AXES, None, None)
    return jax.shard_map(
        local,
        mesh=mesh,
        in_specs=(
            split, P(), P(), P(), P(), P(), P(), cube, cube, split, split, P(), split,
        ),
        out_specs=(split, split, P(), P(), P(), P(), P(), P(), cube, cube),
        check_vma=False,
    )
```

profile of v0, /device:TPU:0, one launch (start us, length us, event | category | flops | bytes accessed | tf_op | source)
XLA Modules:
  0.0 319.8 jit_solution(5862687637325779846)
XLA Ops:
  0.6 0.0 copy-start
  0.7 0.7 copy-done
  1.3 0.0 copy-start.4
  1.3 1.4 copy-done.4
  2.7 4.5 %slots.1 = (s32[1,1024]{1,0:T(1,128)S(1)}, s32[1,1024]{1,0:T(1,128)S(1)}, bf16[1280,768]{1,0:T(8,128)(2,1)}) custom-call(s32[1,1024]{1,0:T(1,128)S(1)} %bitcast.18, bf16[1024,768]{1,0:T(8,128)(2,1)S(1)} %copy-done.4), custom_call_target="tpu_custom_call" | custom-call | flops 5750000128 | bytes 4194304 | tf_op jit(solution)/shard_map/slots/pallas_call | solution.py:79
  7.3 0.0 copy-start.2
  7.3 0.6 copy-done.2
  7.9 0.0 copy-start.5
  7.9 0.6 copy-done.5
  8.5 0.0 copy-start.8
  8.5 0.0 copy-start.9
  8.5 7.3 %all-to-all-start = ((bf16[32,40,768]{2,1,0:T(8,128)(2,1)}), bf16[32,40,768]{2,1,0:T(8,128)(2,1)S(1)}, u32[]{:S(2)}, u32[]{:S(2)}) async-start(bf16[32,40,768]{2,1,0:T(8,128)(2,1)} %bitcast.4), calls=%async_computation | async-start | bytes 3932160 | tf_op jit(solution)/shard_map/all_to_all | solution.py:1241
  15.8 0.0 copy-done.8
  15.8 0.6 reshape.193.gain1_ref
  16.4 0.0 copy-done.9
  16.4 0.6 reshape.194.gain2_ref
  17.0 49.5 %front.1 = (bf16[768,1024]{1,0:T(8,128)(2,1)}, bf16[768,1024]{1,0:T(8,128)(2,1)}, bf16[768,1024]{1,0:T(8,128)(2,1)}, bf16[768,1024]{1,0:T(8,128)(2,1)}, bf16[12,...) custom-call(bf16[1024,768]{1,0:T(8,128)(2,1)} %hid_any.1, ...), custom_call_target="tpu_custom_call" | custom-call | flops 57500000256 | bytes 31457280 | tf_op jit(solution)/shard_map/front/pallas_call | solution.py:202
  66.5 0.0 all-to-all-done.grows
  66.5 0.0 copy-start.6
  66.5 1.3 copy-done.6
  67.8 78.0 %expert.1 = (bf16[1280,768]{1,0:T(8,128)(2,1)}, bf16[16,40,768]{2,1,0:T(8,128)(2,1)}, bf16[16,40,768]{2,1,0:T(8,128)(2,1)}, bf16[1280,3072]{1,0:T(8,128)(2,1)}, ...) custom-call(bf16[32,40,768]{2,1,0:T(8,128)(2,1)} %bitcast.27, ...), custom_call_target="tpu_custom_call" | custom-call | flops 69000003584 | bytes 62914560 | tf_op jit(solution)/shard_map/expert/pallas_call | solution.py:503
  145.7 0.0 copy-start.7
  145.8 8.0 %all-to-all-start.1 = ((bf16[32,40,768]{2,1,0:T(8,128)(2,1)}), bf16[32,40,768]{2,1,0:T(8,128)(2,1)}, u32[]{:S(2)}, u32[]{:S(2)}) async-start(bf16[32,40,768]{2,1,0:T(8,128)(2,1)} %bitcast.19), calls=%async_computation.1 | async-start | bytes 3932160 | tf_op jit(solution)/shard_map/all_to_all | solution.py:1241
  153.7 0.0 copy-done.7
  153.8 0.0 copy-start.1
  153.8 0.0 copy-start.3
  153.8 1.3 copy.23
  155.1 0.0 copy-done.1
  155.1 0.0 copy-done.3
  155.1 0.6 compare_select_fusion.2.slot_ref
  155.7 20.8 %weight_grads.1 = (f32[1,3072,768]{2,1,0:T(8,128)}, f32[1,768,3072]{2,1,0:T(8,128)}) custom-call(bf16[1280,3072]{1,0:T(8,128)(2,1)} %get-tuple-element.59.active_ref, bf16[1280,768]{1,0:T(8,128)(2,1)} %get-tuple-element.60.gs_ref, bf16[1280,768]{1,0:T(8,128)(2,1)} %bitcast.26, bf16[1280,3072]{1,0:T(8,128)(2,1)} %get-tuple-element.62.ginner_ref), custom_call_target="tpu_custom_call" | custom-call | flops 20700000256 | bytes 37748736 | tf_op jit(solution)/shard_map/weight_grads/pallas_call | solution.py:547
  176.5 24.5 %all-to-all-done.1 = bf16[32,40,768]{2,1,0:T(8,128)(2,1)} async-done(((bf16[32,40,768]{2,1,0:T(8,128)(2,1)}), bf16[32,40,768]{2,1,0:T(8,128)(2,1)}, u32[]{:S(2)}, u32[]{:S(2)}) %all-to-all-start.1) | async-done | bytes 1966112 | tf_op jit(solution)/shard_map/all_to_all | solution.py:1241
  201.1 107.1 %back.1 = (f32[768,1024]{1,0:T(8,128)}, bf16[16,40,768]{2,1,0:T(8,128)(2,1)}, bf16[2,2,32,24,384]{4,3,2,1,0:T(8,128)(2,1)}, bf16[3,2,32,24,256]{4,3,2,1,0:T(8,12...) custom-call(bf16[1280,768]{1,0:T(8,128)(2,1)} %bitcast.9.dx_ref, bf16[32,8,128]{2,1,0:T(8,128)(2,1)} %get-tuple-element.66.gg_ref, ...), custom_call_target="tpu_custom_call" | custom-call | flops 92000002048 | bytes 52428800 | tf_op jit(solution)/shard_map/back/pallas_call | solution.py:1114
  308.2 11.4 %finish.1 = (bf16[1024,768]{1,0:T(8,128)(2,1)}, f32[768,2304]{1,0:T(8,128)}, f32[768,768]{1,0:T(8,128)}, f32[1024,768]{1,0:T(8,128)}, f32[768]{0:T(1024)}, /*ind...) custom-call(bf16[640,768]{1,0:T(8,128)(2,1)} %bitcast.28, bf16[640,768]{1,0:T(8,128)(2,1)} %bitcast.29, ...), custom_call_target="tpu_custom_call" | custom-call | flops 9200000000 | bytes 20971520 | tf_op jit(solution)/shard_map/finish/pallas_call | solution.py:1202
Async XLA Ops:
  0.6 0.7 copy-start
  1.3 1.4 copy-start.4
  7.3 0.6 copy-start.2
  7.9 0.6 copy-start.5
  8.5 7.3 %copy-start.8 = (f32[768]{0:T(1024)S(1)}, f32[768]{0:T(1024)}, u32[]{:S(2)}) copy-start(f32[768]{0:T(1024)} %param.14) | copy-start | bytes 9220
  8.5 7.9 %copy-start.9 = (f32[768]{0:T(1024)S(1)}, f32[768]{0:T(1024)}, u32[]{:S(2)}) copy-start(f32[768]{0:T(1024)} %param.18) | copy-start | bytes 9220
  8.5 58.0 %all-to-all-start = ((bf16[32,40,768]{2,1,0:T(8,128)(2,1)}), bf16[32,40,768]{2,1,0:T(8,128)(2,1)S(1)}, u32[]{:S(2)}, u32[]{:S(2)}) async-start(bf16[32,40,768]{2,1,0:T(8,128)(2,1)} %bitcast.4), calls=%async_computation | async-start | bytes 3932160 | tf_op jit(solution)/shard_map/all_to_all | solution.py:1241
  66.5 1.3 copy-start.6
  145.7 8.0 %copy-start.7 = (s32[512,512]{1,0:T(8,128)S(1)}, s32[512,512]{1,0:T(8,128)}, u32[]{:S(2)}) copy-start(s32[512,512]{1,0:T(8,128)} %rel_ref.1) | copy-start | bytes 3145732
  145.8 55.3 %all-to-all-start.1 = ((bf16[32,40,768]{2,1,0:T(8,128)(2,1)}), bf16[32,40,768]{2,1,0:T(8,128)(2,1)}, u32[]{:S(2)}, u32[]{:S(2)}) async-start(bf16[32,40,768]{2,1,0:T(8,128)(2,1)} %bitcast.19), calls=%async_computation.1 | async-start | bytes 3932160 | tf_op jit(solution)/shard_map/all_to_all | solution.py:1241
  153.8 1.3 copy-start.1
  153.8 1.3 copy-start.3
where the time goes:
time: 321 us; the launch traced here: 320 us
  Pallas kernels  271 us (84%)
  waiting for transfers between devices  24.5 us (8%)
  starting transfers between devices  15.3 us (5%)
  local copies, waits for them, and re-layouts  7.05 us (2%)
    pallas_call x1, Pallas kernels, back(): pl.pallas_call(functools.partial(back_kernel, block), grid=(GROUPS, GROUP...  107 us
    pallas_call x1, Pallas kernels, expert(): pl.pallas_call(functools.partial(expert_kernel, block), in_specs=[anyspec...  78 us
    pallas_call x1, Pallas kernels, front(): pl.pallas_call(front_kernel, grid=(GROUPS,), in_specs=[whole((tok, width)...  49.5 us
    all_to_all x2, waiting for transfers between devices, exchange(): return lax.all_to_all(v, AXES, split_axis=0, concat_axis=0, tiled=True)  24.5 us
    pallas_call x1, Pallas kernels, weight_grads(): pl.pallas_call(weights_kernel, grid=(hidden // tile,), in_specs=[cols, wh...  20.8 us
    all_to_all x2, starting transfers between devices, exchange(): return lax.all_to_all(v, AXES, split_axis=0, concat_axis=0, tiled=True)  15.3 us
    pallas_call x1, Pallas kernels, finish(): pl.pallas_call(finish_kernel, grid=(steps,), in_specs=[whole(out_a.shape)...  11.4 us
  transfers between devices with their start and end apart: 2, of which 1 were waited for; matrix products, arithmetic and copies ran while one was open for 1% of the time, Pallas kernels for 22%

commit v1 on v0

--- a/solution.py
+++ b/solution.py
@@ -1082,10 +1082,10 @@
 EARLY_MOST = 64
 EARLY_LEVELS = (1, 3, 5, 7, 9)
 SCHEDULE = (
-    [(0, phase, at) for phase, at in enumerate((0, 2, 4, 6, 8, 10))]
-    + [(1, phase, at) for phase, at in enumerate((1, 3, 5, 8, 11))]
-    + [(2, phase, at) for phase, at in enumerate((5, 7, 10))]
-    + [(3, phase, at) for phase, at in enumerate((9, 11))]
+    [(0, phase, at) for phase, at in enumerate((1, 3, 5, 7, 9, 11))]
+    + [(1, phase, at) for phase, at in enumerate((3, 6, 9))]
+    + [(2, phase, at) for phase, at in enumerate((6, 8, 11))]
+    + [(3, phase, at) for phase, at in enumerate((10,))]
 )
 
 

time: 321 us -> 316 us (0.984)
  Pallas kernels: 271 us -> 267 us
    pallas_call x1, Pallas kernels: 107 us -> 103 us  [back(): pl.pallas_call(functools.partial(back_kernel, block), grid=(GROUPS, GROUP...]
where the time goes in v1:
time: 316 us; the launch traced here: 315 us
  Pallas kernels  267 us (84%)
  waiting for transfers between devices  24.5 us (8%)
  starting transfers between devices  15.3 us (5%)
  local copies, waits for them, and re-layouts  7.05 us (2%)
    pallas_call x1, Pallas kernels, back(): pl.pallas_call(functools.partial(back_kernel, block), grid=(GROUPS, GROUP...  103 us
    pallas_call x1, Pallas kernels, expert(): pl.pallas_call(functools.partial(expert_kernel, block), in_specs=[anyspec...  78 us
    pallas_call x1, Pallas kernels, front(): pl.pallas_call(front_kernel, grid=(GROUPS,), in_specs=[whole((tok, width)...  49.5 us
    all_to_all x2, waiting for transfers between devices, exchange(): return lax.all_to_all(v, AXES, split_axis=0, concat_axis=0, tiled=True)  24.5 us
    pallas_call x1, Pallas kernels, weight_grads(): pl.pallas_call(weights_kernel, grid=(hidden // tile,), in_specs=[cols, wh...  20.8 us
    all_to_all x2, starting transfers between devices, exchange(): return lax.all_to_all(v, AXES, split_axis=0, concat_axis=0, tiled=True)  15.3 us
    pallas_call x1, Pallas kernels, finish(): pl.pallas_call(finish_kernel, grid=(steps,), in_specs=[whole(out_a.shape)...  11.4 us
  transfers between devices with their start and end apart: 2, of which 1 were waited for; matrix products, arithmetic and copies ran while one was open for 1% of the time, Pallas kernels for 22%

profile of v1, /device:TPU:0, one launch (start us, length us, event | category | flops | bytes accessed | tf_op | source)
XLA Modules:
  0.0 315.4 jit_solution(16075792037841282494)
XLA Ops:
  0.6 0.0 copy-start
  0.7 0.7 copy-done
  1.3 0.0 copy-start.4
  1.3 1.4 copy-done.4
  2.7 4.5 %slots.1 = (s32[1,1024]{1,0:T(1,128)S(1)}, s32[1,1024]{1,0:T(1,128)S(1)}, bf16[1280,768]{1,0:T(8,128)(2,1)}) custom-call(s32[1,1024]{1,0:T(1,128)S(1)} %bitcast.18, bf16[1024,768]{1,0:T(8,128)(2,1)S(1)} %copy-done.4), custom_call_target="tpu_custom_call" | custom-call | flops 5750000128 | bytes 4194304 | tf_op jit(solution)/shard_map/slots/pallas_call | solution.py:79
  7.3 0.0 copy-start.2
  7.3 0.6 copy-done.2
  7.9 0.0 copy-start.5
  7.9 0.6 copy-done.5
  8.5 0.0 copy-start.8
  8.5 0.0 copy-start.9
  8.5 7.3 %all-to-all-start = ((bf16[32,40,768]{2,1,0:T(8,128)(2,1)}), bf16[32,40,768]{2,1,0:T(8,128)(2,1)S(1)}, u32[]{:S(2)}, u32[]{:S(2)}) async-start(bf16[32,40,768]{2,1,0:T(8,128)(2,1)} %bitcast.4), calls=%async_computation | async-start | bytes 3932160 | tf_op jit(solution)/shard_map/all_to_all | solution.py:1241
  15.8 0.0 copy-done.8
  15.8 0.6 reshape.193.gain1_ref
  16.4 0.0 copy-done.9
  16.4 0.6 reshape.194.gain2_ref
  17.0 49.5 %front.1 = (bf16[768,1024]{1,0:T(8,128)(2,1)}, bf16[768,1024]{1,0:T(8,128)(2,1)}, bf16[768,1024]{1,0:T(8,128)(2,1)}, bf16[768,1024]{1,0:T(8,128)(2,1)}, bf16[12,...) custom-call(bf16[1024,768]{1,0:T(8,128)(2,1)} %hid_any.1, ...), custom_call_target="tpu_custom_call" | custom-call | flops 57500000256 | bytes 31457280 | tf_op jit(solution)/shard_map/front/pallas_call | solution.py:202
  66.5 0.0 all-to-all-done.grows
  66.5 0.0 copy-start.6
  66.5 1.3 copy-done.6
  67.8 78.0 %expert.1 = (bf16[1280,768]{1,0:T(8,128)(2,1)}, bf16[16,40,768]{2,1,0:T(8,128)(2,1)}, bf16[16,40,768]{2,1,0:T(8,128)(2,1)}, bf16[1280,3072]{1,0:T(8,128)(2,1)}, ...) custom-call(bf16[32,40,768]{2,1,0:T(8,128)(2,1)} %bitcast.27, ...), custom_call_target="tpu_custom_call" | custom-call | flops 69000003584 | bytes 62914560 | tf_op jit(solution)/shard_map/expert/pallas_call | solution.py:503
  145.7 0.0 copy-start.7
  145.8 8.0 %all-to-all-start.1 = ((bf16[32,40,768]{2,1,0:T(8,128)(2,1)}), bf16[32,40,768]{2,1,0:T(8,128)(2,1)}, u32[]{:S(2)}, u32[]{:S(2)}) async-start(bf16[32,40,768]{2,1,0:T(8,128)(2,1)} %bitcast.19), calls=%async_computation.1 | async-start | bytes 3932160 | tf_op jit(solution)/shard_map/all_to_all | solution.py:1241
  153.7 0.0 copy-done.7
  153.8 0.0 copy-start.1
  153.8 0.0 copy-start.3
  153.8 1.3 copy.23
  155.1 0.0 copy-done.1
  155.1 0.0 copy-done.3
  155.1 0.6 compare_select_fusion.2.slot_ref
  155.7 20.8 %weight_grads.1 = (f32[1,3072,768]{2,1,0:T(8,128)}, f32[1,768,3072]{2,1,0:T(8,128)}) custom-call(bf16[1280,3072]{1,0:T(8,128)(2,1)} %get-tuple-element.59.active_ref, bf16[1280,768]{1,0:T(8,128)(2,1)} %get-tuple-element.60.gs_ref, bf16[1280,768]{1,0:T(8,128)(2,1)} %bitcast.26, bf16[1280,3072]{1,0:T(8,128)(2,1)} %get-tuple-element.62.ginner_ref), custom_call_target="tpu_custom_call" | custom-call | flops 20700000256 | bytes 37748736 | tf_op jit(solution)/shard_map/weight_grads/pallas_call | solution.py:547
  176.5 24.5 %all-to-all-done.1 = bf16[32,40,768]{2,1,0:T(8,128)(2,1)} async-done(((bf16[32,40,768]{2,1,0:T(8,128)(2,1)}), bf16[32,40,768]{2,1,0:T(8,128)(2,1)}, u32[]{:S(2)}, u32[]{:S(2)}) %all-to-all-start.1) | async-done | bytes 1966112 | tf_op jit(solution)/shard_map/all_to_all | solution.py:1241
  201.1 102.7 %back.1 = (f32[768,1024]{1,0:T(8,128)}, bf16[16,40,768]{2,1,0:T(8,128)(2,1)}, bf16[2,2,32,24,384]{4,3,2,1,0:T(8,128)(2,1)}, bf16[3,2,32,24,256]{4,3,2,1,0:T(8,12...) custom-call(bf16[1280,768]{1,0:T(8,128)(2,1)} %bitcast.9.dx_ref, bf16[32,8,128]{2,1,0:T(8,128)(2,1)} %get-tuple-element.66.gg_ref, ...), custom_call_target="tpu_custom_call" | custom-call | flops 92000002048 | bytes 52428800 | tf_op jit(solution)/shard_map/back/pallas_call | solution.py:1114
  303.8 11.4 %finish.1 = (bf16[1024,768]{1,0:T(8,128)(2,1)}, f32[768,2304]{1,0:T(8,128)}, f32[768,768]{1,0:T(8,128)}, f32[1024,768]{1,0:T(8,128)}, f32[768]{0:T(1024)}, /*ind...) custom-call(bf16[640,768]{1,0:T(8,128)(2,1)} %bitcast.28, bf16[640,768]{1,0:T(8,128)(2,1)} %bitcast.29, ...), custom_call_target="tpu_custom_call" | custom-call | flops 9200000000 | bytes 20971520 | tf_op jit(solution)/shard_map/finish/pallas_call | solution.py:1202
Async XLA Ops:
  0.6 0.7 copy-start
  1.3 1.4 copy-start.4
  7.3 0.6 copy-start.2
  7.9 0.6 copy-start.5
  8.5 7.3 %copy-start.8 = (f32[768]{0:T(1024)S(1)}, f32[768]{0:T(1024)}, u32[]{:S(2)}) copy-start(f32[768]{0:T(1024)} %param.14) | copy-start | bytes 9220
  8.5 7.9 %copy-start.9 = (f32[768]{0:T(1024)S(1)}, f32[768]{0:T(1024)}, u32[]{:S(2)}) copy-start(f32[768]{0:T(1024)} %param.18) | copy-start | bytes 9220
  8.5 58.0 %all-to-all-start = ((bf16[32,40,768]{2,1,0:T(8,128)(2,1)}), bf16[32,40,768]{2,1,0:T(8,128)(2,1)S(1)}, u32[]{:S(2)}, u32[]{:S(2)}) async-start(bf16[32,40,768]{2,1,0:T(8,128)(2,1)} %bitcast.4), calls=%async_computation | async-start | bytes 3932160 | tf_op jit(solution)/shard_map/all_to_all | solution.py:1241
  66.5 1.3 copy-start.6
  145.7 8.0 %copy-start.7 = (s32[512,512]{1,0:T(8,128)S(1)}, s32[512,512]{1,0:T(8,128)}, u32[]{:S(2)}) copy-start(s32[512,512]{1,0:T(8,128)} %rel_ref.1) | copy-start | bytes 3145732
  145.8 55.3 %all-to-all-start.1 = ((bf16[32,40,768]{2,1,0:T(8,128)(2,1)}), bf16[32,40,768]{2,1,0:T(8,128)(2,1)}, u32[]{:S(2)}, u32[]{:S(2)}) async-start(bf16[32,40,768]{2,1,0:T(8,128)(2,1)} %bitcast.19), calls=%async_computation.1 | async-start | bytes 3932160 | tf_op jit(solution)/shard_map/all_to_all | solution.py:1241
  153.8 1.3 copy-start.1
  153.8 1.3 copy-start.3

commit v2 on v1

--- a/solution.py
+++ b/solution.py
@@ -1083,9 +1083,9 @@
 EARLY_LEVELS = (1, 3, 5, 7, 9)
 SCHEDULE = (
     [(0, phase, at) for phase, at in enumerate((1, 3, 5, 7, 9, 11))]
-    + [(1, phase, at) for phase, at in enumerate((3, 6, 9))]
-    + [(2, phase, at) for phase, at in enumerate((6, 8, 11))]
-    + [(3, phase, at) for phase, at in enumerate((10,))]
+    + [(1, phase, at) for phase, at in enumerate((3, 5, 7, 9, 11))]
+    + [(2, phase, at) for phase, at in enumerate((7, 9, 11))]
+    + [(3, phase, at) for phase, at in enumerate((11,))]
 )
 
 

time: 316 us -> 319 us (level)
  no operation moved by 1% of the time
where the time goes in v2:
time: 319 us; the launch traced here: 318 us
  Pallas kernels  269 us (84%)
  waiting for transfers between devices  24.5 us (8%)
  starting transfers between devices  15.3 us (5%)
  local copies, waits for them, and re-layouts  7.05 us (2%)
    pallas_call x1, Pallas kernels, back(): pl.pallas_call(functools.partial(back_kernel, block), grid=(GROUPS, GROUP...  105 us
    pallas_call x1, Pallas kernels, expert(): pl.pallas_call(functools.partial(expert_kernel, block), in_specs=[anyspec...  78 us
    pallas_call x1, Pallas kernels, front(): pl.pallas_call(front_kernel, grid=(GROUPS,), in_specs=[whole((tok, width)...  49.5 us
    all_to_all x2, waiting for transfers between devices, exchange(): return lax.all_to_all(v, AXES, split_axis=0, concat_axis=0, tiled=True)  24.5 us
    pallas_call x1, Pallas kernels, weight_grads(): pl.pallas_call(weights_kernel, grid=(hidden // tile,), in_specs=[cols, wh...  20.8 us
    all_to_all x2, starting transfers between devices, exchange(): return lax.all_to_all(v, AXES, split_axis=0, concat_axis=0, tiled=True)  15.3 us
    pallas_call x1, Pallas kernels, finish(): pl.pallas_call(finish_kernel, grid=(steps,), in_specs=[whole(out_a.shape)...  11.4 us
  transfers between devices with their start and end apart: 2, of which 1 were waited for; matrix products, arithmetic and copies ran while one was open for 1% of the time, Pallas kernels for 22%

profile of v2, /device:TPU:0, one launch (start us, length us, event | category | flops | bytes accessed | tf_op | source)
XLA Modules:
  0.0 317.9 jit_solution(1399846055761618457)
XLA Ops:
  0.6 0.0 copy-start
  0.7 0.7 copy-done
  1.3 0.0 copy-start.4
  1.3 1.4 copy-done.4
  2.7 4.5 %slots.1 = (s32[1,1024]{1,0:T(1,128)S(1)}, s32[1,1024]{1,0:T(1,128)S(1)}, bf16[1280,768]{1,0:T(8,128)(2,1)}) custom-call(s32[1,1024]{1,0:T(1,128)S(1)} %bitcast.18, bf16[1024,768]{1,0:T(8,128)(2,1)S(1)} %copy-done.4), custom_call_target="tpu_custom_call" | custom-call | flops 5750000128 | bytes 4194304 | tf_op jit(solution)/shard_map/slots/pallas_call | solution.py:79
  7.3 0.0 copy-start.2
  7.3 0.6 copy-done.2
  7.9 0.0 copy-start.5
  7.9 0.6 copy-done.5
  8.5 0.0 copy-start.8
  8.5 0.0 copy-start.9
  8.5 7.3 %all-to-all-start = ((bf16[32,40,768]{2,1,0:T(8,128)(2,1)}), bf16[32,40,768]{2,1,0:T(8,128)(2,1)S(1)}, u32[]{:S(2)}, u32[]{:S(2)}) async-start(bf16[32,40,768]{2,1,0:T(8,128)(2,1)} %bitcast.4), calls=%async_computation | async-start | bytes 3932160 | tf_op jit(solution)/shard_map/all_to_all | solution.py:1241
  15.8 0.0 copy-done.8
  15.8 0.6 reshape.193.gain1_ref
  16.4 0.0 copy-done.9
  16.4 0.6 reshape.194.gain2_ref
  17.0 49.5 %front.1 = (bf16[768,1024]{1,0:T(8,128)(2,1)}, bf16[768,1024]{1,0:T(8,128)(2,1)}, bf16[768,1024]{1,0:T(8,128)(2,1)}, bf16[768,1024]{1,0:T(8,128)(2,1)}, bf16[12,...) custom-call(bf16[1024,768]{1,0:T(8,128)(2,1)} %hid_any.1, ...), custom_call_target="tpu_custom_call" | custom-call | flops 57500000256 | bytes 31457280 | tf_op jit(solution)/shard_map/front/pallas_call | solution.py:202
  66.5 0.0 all-to-all-done.grows
  66.5 0.0 copy-start.6
  66.5 1.3 copy-done.6
  67.8 78.0 %expert.1 = (bf16[1280,768]{1,0:T(8,128)(2,1)}, bf16[16,40,768]{2,1,0:T(8,128)(2,1)}, bf16[16,40,768]{2,1,0:T(8,128)(2,1)}, bf16[1280,3072]{1,0:T(8,128)(2,1)}, ...) custom-call(bf16[32,40,768]{2,1,0:T(8,128)(2,1)} %bitcast.27, ...), custom_call_target="tpu_custom_call" | custom-call | flops 69000003584 | bytes 62914560 | tf_op jit(solution)/shard_map/expert/pallas_call | solution.py:503
  145.7 0.0 copy-start.7
  145.8 8.0 %all-to-all-start.1 = ((bf16[32,40,768]{2,1,0:T(8,128)(2,1)}), bf16[32,40,768]{2,1,0:T(8,128)(2,1)}, u32[]{:S(2)}, u32[]{:S(2)}) async-start(bf16[32,40,768]{2,1,0:T(8,128)(2,1)} %bitcast.19), calls=%async_computation.1 | async-start | bytes 3932160 | tf_op jit(solution)/shard_map/all_to_all | solution.py:1241
  153.7 0.0 copy-done.7
  153.8 0.0 copy-start.1
  153.8 0.0 copy-start.3
  153.8 1.3 copy.23
  155.1 0.0 copy-done.1
  155.1 0.0 copy-done.3
  155.1 0.6 compare_select_fusion.2.slot_ref
  155.7 20.8 %weight_grads.1 = (f32[1,3072,768]{2,1,0:T(8,128)}, f32[1,768,3072]{2,1,0:T(8,128)}) custom-call(bf16[1280,3072]{1,0:T(8,128)(2,1)} %get-tuple-element.59.active_ref, bf16[1280,768]{1,0:T(8,128)(2,1)} %get-tuple-element.60.gs_ref, bf16[1280,768]{1,0:T(8,128)(2,1)} %bitcast.26, bf16[1280,3072]{1,0:T(8,128)(2,1)} %get-tuple-element.62.ginner_ref), custom_call_target="tpu_custom_call" | custom-call | flops 20700000256 | bytes 37748736 | tf_op jit(solution)/shard_map/weight_grads/pallas_call | solution.py:547
  176.5 24.5 %all-to-all-done.1 = bf16[32,40,768]{2,1,0:T(8,128)(2,1)} async-done(((bf16[32,40,768]{2,1,0:T(8,128)(2,1)}), bf16[32,40,768]{2,1,0:T(8,128)(2,1)}, u32[]{:S(2)}, u32[]{:S(2)}) %all-to-all-start.1) | async-done | bytes 1966112 | tf_op jit(solution)/shard_map/all_to_all | solution.py:1241
  201.1 105.2 %back.1 = (f32[768,1024]{1,0:T(8,128)}, bf16[16,40,768]{2,1,0:T(8,128)(2,1)}, bf16[2,2,32,24,384]{4,3,2,1,0:T(8,128)(2,1)}, bf16[3,2,32,24,256]{4,3,2,1,0:T(8,12...) custom-call(bf16[1280,768]{1,0:T(8,128)(2,1)} %bitcast.9.dx_ref, bf16[32,8,128]{2,1,0:T(8,128)(2,1)} %get-tuple-element.66.gg_ref, ...), custom_call_target="tpu_custom_call" | custom-call | flops 92000002048 | bytes 52428800 | tf_op jit(solution)/shard_map/back/pallas_call | solution.py:1114
  306.3 11.4 %finish.1 = (bf16[1024,768]{1,0:T(8,128)(2,1)}, f32[768,2304]{1,0:T(8,128)}, f32[768,768]{1,0:T(8,128)}, f32[1024,768]{1,0:T(8,128)}, f32[768]{0:T(1024)}, /*ind...) custom-call(bf16[640,768]{1,0:T(8,128)(2,1)} %bitcast.28, bf16[640,768]{1,0:T(8,128)(2,1)} %bitcast.29, ...), custom_call_target="tpu_custom_call" | custom-call | flops 9200000000 | bytes 20971520 | tf_op jit(solution)/shard_map/finish/pallas_call | solution.py:1202
Async XLA Ops:
  0.6 0.7 copy-start
  1.3 1.4 copy-start.4
  7.3 0.6 copy-start.2
  7.9 0.6 copy-start.5
  8.5 7.3 %copy-start.8 = (f32[768]{0:T(1024)S(1)}, f32[768]{0:T(1024)}, u32[]{:S(2)}) copy-start(f32[768]{0:T(1024)} %param.14) | copy-start | bytes 9220
  8.5 7.9 %copy-start.9 = (f32[768]{0:T(1024)S(1)}, f32[768]{0:T(1024)}, u32[]{:S(2)}) copy-start(f32[768]{0:T(1024)} %param.18) | copy-start | bytes 9220
  8.5 58.0 %all-to-all-start = ((bf16[32,40,768]{2,1,0:T(8,128)(2,1)}), bf16[32,40,768]{2,1,0:T(8,128)(2,1)S(1)}, u32[]{:S(2)}, u32[]{:S(2)}) async-start(bf16[32,40,768]{2,1,0:T(8,128)(2,1)} %bitcast.4), calls=%async_computation | async-start | bytes 3932160 | tf_op jit(solution)/shard_map/all_to_all | solution.py:1241
  66.5 1.3 copy-start.6
  145.7 8.0 %copy-start.7 = (s32[512,512]{1,0:T(8,128)S(1)}, s32[512,512]{1,0:T(8,128)}, u32[]{:S(2)}) copy-start(s32[512,512]{1,0:T(8,128)} %rel_ref.1) | copy-start | bytes 3145732
  145.8 55.3 %all-to-all-start.1 = ((bf16[32,40,768]{2,1,0:T(8,128)(2,1)}), bf16[32,40,768]{2,1,0:T(8,128)(2,1)}, u32[]{:S(2)}, u32[]{:S(2)}) async-start(bf16[32,40,768]{2,1,0:T(8,128)(2,1)} %bitcast.19), calls=%async_computation.1 | async-start | bytes 3932160 | tf_op jit(solution)/shard_map/all_to_all | solution.py:1241
  153.8 1.3 copy-start.1
  153.8 1.3 copy-start.3
